TPU v7x, 32 devices: a whole 2x2x4 slice. The times are simulated.
32 devices in a mesh: geom: 2 (over x), edge: 4 (over y, core), mode: 4 (over z).
Axes of the slice: x: 2, y: 2, z: 4, core: 2. Of those that a mesh axis runs over, the one named last changes fastest.
Arguments:
- basis: bfloat16 [12288, 1024], P(('geom', 'edge'), 'mode'), parts along dimension 0, may hold values from -6 to 6
- motional: bfloat16 [4, 48, 16, 128, 128], P('geom', 'edge'), parts along dimension 0, may hold values from -0.0017089844 to 0.0017089844
- block_cols: int32 [96, 16], P(('geom', 'edge')), parts along dimension 0, may hold values from 0 to 47, as said below
- block_counts: int32 [96], P(('geom', 'edge')), parts along dimension 0, may hold values from 8 to 16, as said below
Outputs:
- reduced: float32 [4, 1024, 1024], P('geom', 'edge', 'mode'), parts along dimension 0
There are 2 independent parts, one for each index of `geom`. A program takes and returns all parts, laid end to end along the dimension named above; each array names one. Nothing has to cross between parts.
Inputs may be any that keep to these rules, and one draw needn't show every extreme that they name: `block_cols`: block row r's live slots hold distinct block columns within 12 blocks of r (at most r + 12, at least r - 12); slot 0 is r itself; slots at or past block_counts[r] hold r. block_counts[r] never exceeds the number of block columns within 12 blocks of r.
All inputs are finite; a program needn't handle non-finite values.
Results may differ from a plain program's by a relative error of at most 0.0029.
Values may be sent and summed in bfloat16 or wider, within the bound.
A program may use at most 64 MiB of HBM per device.

v0:
```python
import jax
import jax.numpy as jnp
from jax import lax
from jax.sharding import PartitionSpec as P


def padded(x, sides, width):
    for axis, dim in sides:
        size, length = (lax.axis_size(axis), x.shape[dim])
        up = [(i, (i + 1) % size) for i in range(size - 1)]
        down = [(j, i) for i, j in up]
        last = lax.slice_in_dim(x, length - width, length, axis=dim)
        initial = lax.slice_in_dim(x, 0, width, axis=dim)
        before = lax.ppermute(last, axis, up)
        after = lax.ppermute(initial, axis, down)
        x = jnp.concatenate([before, x, after], axis=dim)
    return x


def per_device(basis, motional, block_cols, block_counts):
    rows, cols_local = basis.shape
    nbr, nnz = block_cols.shape
    bsize = motional.shape[-1]
    extended = padded(basis, (("edge", 0),), nbr * bsize)
    tiles = extended.reshape(3 * nbr, bsize, cols_local)
    first_block = lax.axis_index("edge") * nbr
    local_cols = block_cols - first_block + nbr
    live = jnp.arange(nnz, dtype=jnp.int32)[None, :] < block_counts[:, None]
    picked = jnp.take(tiles, local_cols, axis=0)
    picked = jnp.where(live[:, :, None, None], picked, jnp.zeros_like(picked))
    work = jnp.einsum("qbkij,bkjm->qbim", motional, picked, preferred_element_type=jnp.float32)
    work = work.astype(jnp.bfloat16).reshape(2, rows, cols_local)
    partial_sum = jnp.einsum(
        "ri,qrj->qij",
        lax.all_gather(basis, "mode", axis=1, tiled=True),
        work,
        preferred_element_type=jnp.float32,
    )
    total = lax.psum(partial_sum, "edge")
    share = total.shape[1] // lax.axis_size("edge")
    return lax.dynamic_slice_in_dim(total, lax.axis_index("edge") * share, share, 1)


def solution(mesh):
    placed = (
        P(("geom", "edge"), "mode"),
        P("geom", "edge", None, None, None),
        P(("geom", "edge"), None),
        P(("geom", "edge")),
    )
    return jax.shard_map(
        per_device, mesh=mesh, in_specs=placed, out_specs=P("geom", "edge", "mode"), check_vma=False
    )
```

profile of v0, /device:TPU:0, one launch (start us, length us, event | category | flops | bytes accessed | tf_op | source)
XLA Modules:
  0.0 138.8 jit_solution(16012564998397765538)
XLA Ops:
  6.5 0.0 all-gather.2.cloned.1.call-start
  6.5 0.7 all-gather.2.cloned.1.call-update
  7.3 0.0 all-reduce.2.cloned.1.call-start
  7.3 2.4 %collective-permute-start = (bf16[1536,256]{1,0:T(8,128)(2,1)}, bf16[1536,256]{1,0:T(8,128)(2,1)S(1)}, u32[]{:S(2)}, u32[]{:S(2)}) collective-permute-start(bf16[1536,256]{1,0:T(8,128)(2,1)} %param.4), channel_id=1, source_target_pairs={{0,4},{4,8},{8,12},{1,5},{5,9},{9,13},{2,6},{6,10},{10,14},{3,7},{... | collective-permute-start | bytes 2359304 | tf_op jit(solution)/shard_map/ppermute | solution.py:14
  9.7 1.3 collective-permute-start.1
  11.0 0.8 compare_and_fusion
  11.8 0.1 reshape.36
  11.9 0.0 collective-permute-done
  11.9 4.4 %collective-permute-done.1 = bf16[1536,256]{1,0:T(8,128)(2,1)} collective-permute-done((bf16[1536,256]{1,0:T(8,128)(2,1)}, bf16[1536,256]{1,0:T(8,128)(2,1)}, u32[]{:S(2)}, u32[]{:S(2)}) %collective-permute-start.1) | collective-permute-done | bytes 786464 | tf_op jit(solution)/shard_map/ppermute | solution.py:15
  16.3 1.5 %pad_maximum_fusion = bf16[4608,256]{1,0:T(8,128)(2,1)S(1)} fusion(bf16[1536,256]{1,0:T(8,128)(2,1)} %collective-permute-done.1, bf16[1536,256]{1,0:T(8,128)(2,1)} %param.4, bf16[1536,256]{1,0:T(8,128)(2,1)S(1)} %collective-permute-done), kind=kLoop, calls=%fused_computation.13 | loop fusion | flops 7077888 | bytes 4718592 | tf_op jit(solution)/shard_map/concatenate | solution.py:16
  17.9 8.2 %gather_fusion = bf16[192,128,256]{2,1,0:T(8,128)(2,1)} fusion(bf16[36,128,256]{2,1,0:T(8,128)(2,1)S(1)} %bitcast.27, s32[1024]{0:T(1024)S(1)} %pad_clamp_fusion), kind=kCustom, calls=%fused_computation | custom fusion | bytes 25166592 | tf_op jit(solution)/shard_map/jit(_take)/gather | solution.py:29
  26.1 10.5 %fusion.18 = bf16[2,12,128,256]{3,2,0,1:T(8,128)(2,1)S(1)} fusion(bf16[2,12,16,128,128]{4,3,2,1,0:T(8,128)(2,1)} %param.5, bf16[12,16,128,256]{3,2,1,0:T(8,128)(2,1)} %bitcast.28, pred[12,16]{1,0:T(8,128)(4,1)S(1)} %get-tuple-element.5, pred[12,16]{1,0:T(8,128)(4,1)S(1)} %get-tuple-element.7), kind=kOutput, calls=%fused_computation.15 | convolution fusion | flops 3234594816 | bytes 26739072 | tf_op jit(solution)/shard_map/qbkij,bkjm->qbim/dot_general | solution.py:31
  36.5 0.1 copy.8
  36.7 38.4 %all-gather.2.cloned.1.call-done = bf16[1536,1024]{1,0:T(8,128)(2,1)} async-done(((bf16[1536,256]{1,0:T(8,128)(2,1)}), bf16[1536,1024]{1,0:T(8,128)(2,1)}) %all-gather.2.cloned.1.call-update) | async-done | bytes 3145744 | tf_op jit(solution)/shard_map/all_gather | solution.py:35
  75.1 5.0 %fusion.15 = f32[2,1024,256]{1,2,0:T(8,128)} fusion(bf16[2,1536,256]{2,1,0:T(8,128)(2,1)S(1)} %bitcast.29, bf16[1536,1024]{1,0:T(8,128)(2,1)} %all-gather.2.cloned.1.call-done), kind=kOutput, calls=%fused_computation.14 | convolution fusion | flops 1610612736 | bytes 6815744 | tf_op jit(solution)/shard_map/ri,qrj->qij/dot_general | solution.py:33
  80.1 0.0 all-reduce.2.cloned.1.call-update
  80.2 49.7 %all-reduce.2.cloned.1.call-done = f32[2,1024,256]{1,2,0:T(8,128)} async-done(((f32[2,1024,256]{1,2,0:T(8,128)}), f32[2,1024,256]{1,2,0:T(8,128)}) %all-reduce.2.cloned.1.call-update) | async-done | bytes 2097168 | tf_op jit(solution)/shard_map/psum | solution.py:39
  129.9 1.1 constant_dynamic-slice_fusion
  130.9 1.0 copy.10
  (1 shorter events, 0.0 us)
Async XLA Ops:
  6.5 68.5 %all-gather.2.cloned.1.call-start = ((), (), s32[]{:S(2)}) async-start(), calls=%async_computation | async-start | bytes 3932160 | tf_op jit(solution)/shard_map/all_gather | solution.py:35
  7.3 122.6 %all-reduce.2.cloned.1.call-start = ((), (), s32[]{:S(2)}) async-start(), calls=%async_computation.1 | async-start | bytes 4194304 | tf_op jit(solution)/shard_map/psum | solution.py:39
  7.3 4.6 %collective-permute-start = (bf16[1536,256]{1,0:T(8,128)(2,1)}, bf16[1536,256]{1,0:T(8,128)(2,1)S(1)}, u32[]{:S(2)}, u32[]{:S(2)}) collective-permute-start(bf16[1536,256]{1,0:T(8,128)(2,1)} %param.4), channel_id=1, source_target_pairs={{0,4},{4,8},{8,12},{1,5},{5,9},{9,13},{2,6},{6,10},{10,14},{3,7},{... | collective-permute-start | bytes 2359304 | tf_op jit(solution)/shard_map/ppermute | solution.py:14
  9.7 6.6 %collective-permute-start.1 = (bf16[1536,256]{1,0:T(8,128)(2,1)}, bf16[1536,256]{1,0:T(8,128)(2,1)}, u32[]{:S(2)}, u32[]{:S(2)}) collective-permute-start(bf16[1536,256]{1,0:T(8,128)(2,1)} %param.4), channel_id=1, source_target_pairs={{4,0},{8,4},{12,8},{5,1},{9,5},{13,9},{6,2},{10,6},{14,10},{7,3},{... | collective-permute-start | bytes 2359304 | tf_op jit(solution)/shard_map/ppermute | solution.py:15
Sparse Core Ops, SparseCore 0:
  8.9 66.1 all-gather.1
  80.3 49.5 all-reduce.1
where the time goes:
time: 139 us
  waiting for transfers between devices  93.2 us (67%)
  matrix products  15.5 us (11%)
  between operations  13.5 us (10%)
  local copies, waits for them, and re-layouts  10.5 us (8%)
  starting transfers between devices  3.74 us (3%)
  other arithmetic  2.31 us (2%)
    psum x1, waiting for transfers between devices, per_device(): total = lax.psum(partial_sum, 'edge')  49.7 us
    all_gather x1, waiting for transfers between devices, per_device(): lax.all_gather(basis, 'mode', axis=1, tiled=True)  38.4 us
    dot_general x1, matrix products, per_device(): jnp.einsum('qbkij,bkjm->qbim', motional, picked, preferred_element_type=j...  10.5 us
    gather x1, local copies, waits for them, and re-layouts, per_device(): picked = jnp.take(tiles, local_cols, axis=0)  8.2 us
    dot_general x1, matrix products, per_device(): jnp.einsum('ri,qrj->qij', lax.all_gather(basis, 'mode', axis=1, tiled=Tru...  5.05 us
    ppermute x1, waiting for transfers between devices, padded(): after = lax.ppermute(initial, axis, down)  4.43 us
  transfers between devices with their start and end apart: 4, of which 3 were waited for; matrix products, arithmetic and copies ran while one was open for 15% of the time, Pallas kernels for 0%

commit v1 on v0

--- a/solution.py
+++ b/solution.py
@@ -36,7 +36,8 @@
         work,
         preferred_element_type=jnp.float32,
     )
-    total = lax.psum(partial_sum, "edge")
+    shards = lax.all_gather(partial_sum, "edge")
+    total = jnp.sum(shards, axis=0)
     share = total.shape[1] // lax.axis_size("edge")
     return lax.dynamic_slice_in_dim(total, lax.axis_index("edge") * share, share, 1)
 

time: 139 us -> 150 us (1.079)
  waiting for transfers between devices: 93.2 us -> 99.1 us
  other arithmetic: 2.31 us -> 6.51 us
  local copies, waits for them, and re-layouts: 10.5 us -> 12.2 us
    all_gather x0 -> x1, waiting for transfers between devices: none -> 56.6 us  [per_device(): shards = lax.all_gather(partial_sum, 'edge')]
    psum x1 -> x0, waiting for transfers between devices: 49.7 us -> none  [per_device(): total = lax.psum(partial_sum, 'edge')]
    reduce_sum x0 -> x1, other arithmetic: none -> 4.21 us  [per_device(): total = jnp.sum(shards, axis=0)]
    transpose x0 -> x1, local copies, waits for them, and re-layouts: none -> 1.86 us  [per_device(): jnp.einsum('ri,qrj->qij', lax.all_gather(basis, 'mode', axis=1, tiled=Tru...]
where the time goes in v1:
time: 150 us
  waiting for transfers between devices  99.1 us (66%)
  matrix products  14.7 us (10%)
  between operations  13.5 us (9%)
  local copies, waits for them, and re-layouts  12.2 us (8%)
  other arithmetic  6.51 us (4%)
  starting transfers between devices  3.74 us (2%)
    all_gather x1, waiting for transfers between devices, per_device(): shards = lax.all_gather(partial_sum, 'edge')  56.6 us
    all_gather x1, waiting for transfers between devices, per_device(): lax.all_gather(basis, 'mode', axis=1, tiled=True)  37.3 us
    dot_general x1, matrix products, per_device(): jnp.einsum('qbkij,bkjm->qbim', motional, picked, preferred_element_type=j...  10.5 us
    gather x1, local copies, waits for them, and re-layouts, per_device(): picked = jnp.take(tiles, local_cols, axis=0)  8.2 us
    ppermute x1, waiting for transfers between devices, padded(): after = lax.ppermute(initial, axis, down)  4.43 us
    reduce_sum x1, other arithmetic, per_device(): total = jnp.sum(shards, axis=0)  4.21 us
    dot_general x1, matrix products, per_device(): jnp.einsum('ri,qrj->qij', lax.all_gather(basis, 'mode', axis=1, tiled=Tru...  4.17 us
  transfers between devices with their start and end apart: 4, of which 3 were waited for; matrix products, arithmetic and copies ran while one was open for 15% of the time, Pallas kernels for 0%

profile of v1, /device:TPU:0, one launch (start us, length us, event | category | flops | bytes accessed | tf_op | source)
XLA Modules:
  0.0 149.6 jit_solution(8080490778399640467)
XLA Ops:
  6.5 0.0 all-gather.4.cloned.1.call-start
  6.5 0.7 all-gather.4.cloned.1.call-update
  7.3 0.0 all-gather.6.cloned.1.call-start
  7.3 2.4 %collective-permute-start = (bf16[1536,256]{1,0:T(8,128)(2,1)}, bf16[1536,256]{1,0:T(8,128)(2,1)S(1)}, u32[]{:S(2)}, u32[]{:S(2)}) collective-permute-start(bf16[1536,256]{1,0:T(8,128)(2,1)} %param.4), channel_id=1, source_target_pairs={{0,4},{4,8},{8,12},{1,5},{5,9},{9,13},{2,6},{6,10},{10,14},{3,7},{... | collective-permute-start | bytes 2359304 | tf_op jit(solution)/shard_map/ppermute | solution.py:14
  9.7 1.3 collective-permute-start.1
  11.0 0.8 compare_and_fusion
  11.8 0.1 reshape.36
  11.9 0.0 collective-permute-done
  11.9 4.4 %collective-permute-done.1 = bf16[1536,256]{1,0:T(8,128)(2,1)} collective-permute-done((bf16[1536,256]{1,0:T(8,128)(2,1)}, bf16[1536,256]{1,0:T(8,128)(2,1)}, u32[]{:S(2)}, u32[]{:S(2)}) %collective-permute-start.1) | collective-permute-done | bytes 786464 | tf_op jit(solution)/shard_map/ppermute | solution.py:15
  16.3 1.5 %pad_maximum_fusion = bf16[4608,256]{1,0:T(8,128)(2,1)S(1)} fusion(bf16[1536,256]{1,0:T(8,128)(2,1)} %collective-permute-done.1, bf16[1536,256]{1,0:T(8,128)(2,1)} %param.4, bf16[1536,256]{1,0:T(8,128)(2,1)S(1)} %collective-permute-done), kind=kLoop, calls=%fused_computation.13 | loop fusion | flops 7077888 | bytes 4718592 | tf_op jit(solution)/shard_map/concatenate | solution.py:16
  17.9 8.2 %gather_fusion = bf16[192,128,256]{2,1,0:T(8,128)(2,1)} fusion(bf16[36,128,256]{2,1,0:T(8,128)(2,1)S(1)} %bitcast.28, s32[1024]{0:T(1024)S(1)} %pad_clamp_fusion), kind=kCustom, calls=%fused_computation | custom fusion | bytes 25166592 | tf_op jit(solution)/shard_map/jit(_take)/gather | solution.py:29
  26.1 10.5 %fusion.18 = bf16[2,12,128,256]{3,2,0,1:T(8,128)(2,1)S(1)} fusion(bf16[2,12,16,128,128]{4,3,2,1,0:T(8,128)(2,1)} %param.5, bf16[12,16,128,256]{3,2,1,0:T(8,128)(2,1)} %bitcast.29, pred[12,16]{1,0:T(8,128)(4,1)S(1)} %get-tuple-element.5, pred[12,16]{1,0:T(8,128)(4,1)S(1)} %get-tuple-element.7), kind=kOutput, calls=%fused_computation.15 | convolution fusion | flops 3234594816 | bytes 26739072 | tf_op jit(solution)/shard_map/qbkij,bkjm->qbim/dot_general | solution.py:31
  36.6 1.3 copy.10
  37.8 37.3 %all-gather.4.cloned.1.call-done = bf16[1536,1024]{1,0:T(8,128)(2,1)} async-done(((bf16[1536,256]{1,0:T(8,128)(2,1)}), bf16[1536,1024]{1,0:T(8,128)(2,1)}) %all-gather.4.cloned.1.call-update) | async-done | bytes 3145744 | tf_op jit(solution)/shard_map/all_gather | solution.py:35
  75.1 4.2 %fusion.15 = f32[2,1024,256]{1,2,0:T(8,128)S(1)} fusion(bf16[2,1536,256]{2,1,0:T(8,128)(2,1)} %bitcast.31, bf16[1536,1024]{1,0:T(8,128)(2,1)} %all-gather.4.cloned.1.call-done), kind=kOutput, calls=%fused_computation.14 | convolution fusion | flops 1610612736 | bytes 6815744 | tf_op jit(solution)/shard_map/ri,qrj->qij/dot_general | solution.py:33
  79.2 1.9 %copy.12 = f32[2,1024,256]{2,1,0:T(8,128)} copy(f32[2,1024,256]{1,2,0:T(8,128)S(1)} %fusion.15) | data formatting | bytes 4194304 | tf_op jit(solution)/shard_map/ri,qrj->qij/transpose | solution.py:33
  81.1 0.0 all-gather.6.cloned.1.call-update
  81.1 56.6 %all-gather.6.cloned.1.call-done = f32[8,1024,256]{2,1,0:T(8,128)} async-done(((f32[2,1024,256]{2,1,0:T(8,128)}), f32[8,1024,256]{2,1,0:T(8,128)}) %all-gather.6.cloned.1.call-update) | async-done | bytes 8388624 | tf_op jit(solution)/shard_map/all_gather | solution.py:39
  137.8 4.2 %reduce_sum.9 = f32[2,1024,256]{2,1,0:T(8,128)S(1)} reduce(f32[4,2,1024,256]{3,2,1,0:T(8,128)} %bitcast.30, f32[]{:T(128)} %constant.31.clone.1), dimensions={0}, to_apply=%region_0.1 | reduce | flops 1572864 | bytes 10485764 | tf_op jit(solution)/shard_map/reduce_sum | solution.py:40
  142.0 0.8 constant_dynamic-slice_fusion
  (1 shorter events, 0.0 us)
Async XLA Ops:
  6.5 68.5 %all-gather.4.cloned.1.call-start = ((), (), s32[]{:S(2)}) async-start(), calls=%async_computation | async-start | bytes 3932160 | tf_op jit(solution)/shard_map/all_gather | solution.py:35
  7.3 130.5 %all-gather.6.cloned.1.call-start = ((), (), s32[]{:S(2)}) async-start(), calls=%async_computation.1 | async-start | bytes 10485760 | tf_op jit(solution)/shard_map/all_gather | solution.py:39
  7.3 4.6 %collective-permute-start = (bf16[1536,256]{1,0:T(8,128)(2,1)}, bf16[1536,256]{1,0:T(8,128)(2,1)S(1)}, u32[]{:S(2)}, u32[]{:S(2)}) collective-permute-start(bf16[1536,256]{1,0:T(8,128)(2,1)} %param.4), channel_id=1, source_target_pairs={{0,4},{4,8},{8,12},{1,5},{5,9},{9,13},{2,6},{6,10},{10,14},{3,7},{... | collective-permute-start | bytes 2359304 | tf_op jit(solution)/shard_map/ppermute | solution.py:14
  9.7 6.6 %collective-permute-start.1 = (bf16[1536,256]{1,0:T(8,128)(2,1)}, bf16[1536,256]{1,0:T(8,128)(2,1)}, u32[]{:S(2)}, u32[]{:S(2)}) collective-permute-start(bf16[1536,256]{1,0:T(8,128)(2,1)} %param.4), channel_id=1, source_target_pairs={{4,0},{8,4},{12,8},{5,1},{9,5},{13,9},{6,2},{10,6},{14,10},{7,3},{... | collective-permute-start | bytes 2359304 | tf_op jit(solution)/shard_map/ppermute | solution.py:15
Sparse Core Ops, SparseCore 0:
  8.9 66.1 all-gather.3
  81.2 56.4 all-gather.5
